TPU v7x, 256 devices: a whole 4x4x8 slice. The times are simulated.
256 devices in a mesh: tm: 16 (over x, z_lo, core), lat: 16 (over z_hi, y).
Axes of the slice: x: 4, y: 4, z: 8 (z_hi: 4, z_lo: 2; z = z_hi * 2 + z_lo), core: 2. Of those that a mesh axis runs over, the one named last changes fastest.
Arguments:
- states: float32 [128, 1024, 256], P('tm', 'lat'), may hold values from -6 to 6
- multipliers: float32 [128, 1024, 256], P('tm', 'lat'), may hold values from -3 to 3
- diffusivity: float32 [1024, 256], P('lat'), may hold values from 0.02 to 0.15
- zonal_speed: float32 [1024, 256], P('lat'), may hold values from -0.3 to 0.3
- meridional_speed: float32 [1024, 256], P('lat'), may hold values from -0.3 to 0.3
- observed_cells: int32 [128, 16, 1024], P('tm', 'lat'), may hold values from 0 to 16383
- observed_values: float32 [128, 16, 1024], P('tm', 'lat'), may hold values from -6 to 6
- observed_weights: float32 [128, 16, 1024], P('tm', 'lat'), may hold values from 0.2 to 2
- fresh_cells: int32 [4, 16, 1024], P(None, 'lat'), may hold values from 0 to 16383
- fresh_values: float32 [4, 16, 1024], P(None, 'lat'), may hold values from -6 to 6
- fresh_weights: float32 [4, 16, 1024], P(None, 'lat'), may hold values from 0.2 to 2
Outputs:
- analysis: float32 [128, 1024, 256], P('tm', 'lat')
- lagrange: float32 [128, 1024, 256], P('tm', 'lat')
Inputs may be any that keep to these rules, and one draw needn't show every extreme that they name: `observed_cells`: each entry names a cell of its band, counted row by row over the band's 64 x 256 cells; cells may repeat. `fresh_cells`: each entry names a cell of its band, counted row by row over the band's 64 x 256 cells; cells may repeat.
All inputs are finite; a program needn't handle non-finite values.
Results may differ from a plain program's by a relative error of at most 0.000059.
Values sent between devices are 32-bit elements; how exact they have to be, the bound alone decides.
A program may use at most 64 MiB of HBM per device.

v0:
```python
import functools

import jax
import jax.numpy as jnp
from jax import lax
from jax.experimental import pallas as pl
from jax.experimental.pallas import tpu as pltpu
from jax.sharding import PartitionSpec as P

MESH = pl.DeviceIdType.MESH
STEP = 0.15
F32 = jnp.float32


def weave(n_tm, n_lat, n_transfers, *refs):
    (
        states,
        mults,
        diff,
        zonal,
        merid,
        cells,
        values,
        weights,
        f_cells,
        f_values,
        f_weights,
        x_out,
        l_out,
        XF,
        LF,
        T1,
        T2,
        CF,
        CB,
        ND,
        NF,
        NB,
        WF,
        VF,
        HX,
        HL,
        E,
        NX,
        NL,
        S7,
        S0,
        SL0,
        PKX,
        PKL,
        SL4,
        RKX,
        RKL,
        OC,
        OV,
        OW,
        ssem,
        rsem,
    ) = refs
    lon = 2 * XF.shape[-1]
    half_lon = lon // 2
    tm = lax.axis_index("tm")
    lat = lax.axis_index("lat")
    made = [0]

    def inside(dt, dl):
        ok = True
        if dt > 0:
            ok = tm < n_tm - 1
        elif dt < 0:
            ok = tm > 0
        if dl > 0:
            ok = jnp.logical_and(ok, lat < n_lat - 1)
        elif dl < 0:
            ok = jnp.logical_and(ok, lat > 0)
        return ok

    class Move:
        def __init__(self, src, dst, dt, dl):
            i = made[0]
            made[0] += 1
            assert i < n_transfers
            self.to, self.by = inside(dt, dl), inside(-dt, -dl)
            self.copy = pltpu.make_async_remote_copy(
                src_ref=src,
                dst_ref=dst,
                send_sem=ssem.at[i],
                recv_sem=rsem.at[i],
                device_id=(tm + dt, lat + dl),
                device_id_type=MESH,
            )
            pl.when(self.to)(self.copy.start)

        def finish(self):
            pl.when(self.to)(self.copy.wait_send)
            pl.when(self.by)(self.copy.wait_recv)

    barrier = pltpu.get_barrier_semaphore()
    greeted = 0
    for dt in (-1, 0, 1):
        for dl in (-1, 0, 1):
            if dt == 0 and dl == 0:
                continue
            ok = inside(dt, dl)

            @pl.when(ok)
            def _():
                pl.semaphore_signal(
                    barrier, inc=1, device_id=(tm + dt, lat + dl), device_id_type=MESH
                )

            greeted = greeted + ok.astype(jnp.int32)

    whole = slice(None)

    def blank(ref, *at):
        ref[at] = jnp.zeros(ref.at[at].shape, ref.dtype)

    @pl.when(lat == 0)
    def _():
        for r in range(4):
            blank(E, r, whole, slice(0, 8))
            blank(NX, r, whole, slice(0, 8))
        for k in range(3):
            blank(ND, k, whole, slice(0, 8))
        blank(NL, 0, whole, slice(0, 8))
        blank(XF, whole, slice(0, 48))
        blank(LF, whole, slice(0, 24))
        blank(RKX, whole, slice(0, 24))

    @pl.when(lat == n_lat - 1)
    def _():
        for r in range(4):
            blank(E, r, whole, slice(72, 80))
            blank(NX, r, whole, slice(72, 80))
        for k in range(3):
            blank(ND, k, whole, slice(72, 80))
        blank(NL, 0, whole, slice(72, 80))
        blank(XF, whole, slice(560, 608))
        blank(LF, whole, slice(536, 560))
        blank(RKX, whole, slice(280, 304))

    @pl.when(tm == 0)
    def _():
        blank(E, 0)
        blank(E, 1)

    @pl.when(tm == n_tm - 1)
    def _():
        for r in range(4):
            blank(NX, r)
        blank(NL, 0)
        blank(NL, 1)

    blank(XF, whole, slice(608, 640))
    blank(LF, whole, slice(560, 576))

    def split(x):
        return jnp.stack([x[:, :half_lon], x[:, half_lon:]])

    def join(x):
        return jnp.concatenate([x[0], x[1]], axis=1)

    for s in range(8):
        XF[:, pl.ds(48 + s, 64, stride=8), :] = split(states[s])
        LF[:, pl.ds(24 + s, 64, stride=8), :] = split(mults[s])
    S7[0] = split(states[7])
    S0[0] = split(states[0])
    SL0[...] = split(mults[0])
    for k, ref in enumerate((diff, zonal, merid)):
        ND[k, :, pl.ds(8, 64), :] = split(ref[...])

    pl.semaphore_wait(barrier, greeted)

    def send_after(r):
        return [
            Move(S0.at[r], NX.at[r, :, pl.ds(8, 64)], -1, 0),
            Move(S0.at[r, :, pl.ds(0, 8)], NX.at[r, :, pl.ds(72, 8)], -1, -1),
            Move(S0.at[r, :, pl.ds(56, 8)], NX.at[r, :, pl.ds(0, 8)], -1, 1),
        ]

    def send_before(r):
        return [
            Move(S7.at[r], E.at[r, :, pl.ds(8, 64)], 1, 0),
            Move(S7.at[r, :, pl.ds(0, 8)], E.at[r, :, pl.ds(72, 8)], 1, -1),
            Move(S7.at[r, :, pl.ds(56, 8)], E.at[r, :, pl.ds(0, 8)], 1, 1),
        ]

    def send_rows(r):
        return [
            Move(XF.at[:, pl.ds(48, 48)], HX.at[r, 1], 0, -1),
            Move(XF.at[:, pl.ds(512, 48)], HX.at[r, 0], 0, 1),
        ]

    def finish(moves):
        for move in moves:
            move.finish()

    def take_rows(r):
        @pl.when(lat > 0)
        def _():
            XF[:, pl.ds(0, 48), :] = HX[r, 0]

        @pl.when(lat < n_lat - 1)
        def _():
            XF[:, pl.ds(560, 48), :] = HX[r, 1]

    def edges(r):
        S7[r] = XF[:, pl.ds(55, 64, stride=8), :]
        S0[r] = XF[:, pl.ds(48, 64, stride=8), :]

    moves = send_rows(0)
    moves += [
        Move(LF.at[:, pl.ds(24, 24)], HL.at[1], 0, -1),
        Move(LF.at[:, pl.ds(512, 24)], HL.at[0], 0, 1),
    ]
    moves += [
        Move(ND.at[:, :, pl.ds(8, 8)], ND.at[:, :, pl.ds(72, 8)], 0, -1),
        Move(ND.at[:, :, pl.ds(64, 8)], ND.at[:, :, pl.ds(0, 8)], 0, 1),
    ]
    moves += send_before(0) + send_after(0)
    moves += [
        Move(SL0, NL.at[0, :, pl.ds(8, 64)], -1, 0),
        Move(SL0.at[:, pl.ds(0, 8)], NL.at[0, :, pl.ds(72, 8)], -1, -1),
        Move(SL0.at[:, pl.ds(56, 8)], NL.at[0, :, pl.ds(0, 8)], -1, 1),
    ]
    obs_moves = [
        Move(cells.at[pl.ds(0, 4)], OC, -1, 0),
        Move(values.at[pl.ds(0, 4)], OV, -1, 0),
        Move(weights.at[pl.ds(0, 4)], OW, -1, 0),
    ]

    n_obs = cells.shape[-1]

    def tables(c, y, w):
        row = lax.shift_right_logical(c, 8)
        column = lax.bitwise_and(c, 255)
        on_row = lax.broadcasted_iota(jnp.int32, (64, n_obs), 0) == row
        on_column = lax.broadcasted_iota(jnp.int32, (lon, n_obs), 0) == column
        wy = w * y
        parts = []
        for full in (w, wy):
            high = full.astype(jnp.bfloat16).astype(F32)
            for part in (high, full - high):
                parts.append(jnp.where(on_row, part, 0.0).astype(jnp.bfloat16))
        left = jnp.concatenate(parts, axis=0)
        right = jnp.where(on_column, 1.0, 0.0).astype(jnp.bfloat16)
        out = lax.dot_general(
            left, right, (((1,), (1,)), ((), ())), preferred_element_type=F32
        )
        return split(out[0:64] + out[64:128]), split(out[128:192] + out[192:256])

    def own_slot(s, carry):
        w, v = tables(cells[s], values[s], weights[s])
        WF[0, :, pl.ds(s, 64, stride=8), :] = w
        VF[0, :, pl.ds(s, 64, stride=8), :] = v
        return carry

    def kept_slot(s, carry):
        w, v = tables(cells[s + 4], values[s + 4], weights[s + 4])
        WF[0, :, pl.ds(s + 4, 64, stride=8), :] = w
        VF[0, :, pl.ds(s + 4, 64, stride=8), :] = v
        WF[1, :, pl.ds(s, 64, stride=8), :] = w
        VF[1, :, pl.ds(s, 64, stride=8), :] = v
        return carry

    def late_slot(s, carry):
        last = tm == n_tm - 1
        w, v = tables(
            jnp.where(last, f_cells[s], OC[s]),
            jnp.where(last, f_values[s], OV[s]),
            jnp.where(last, f_weights[s], OW[s]),
        )
        WF[1, :, pl.ds(s + 4, 64, stride=8), :] = w
        VF[1, :, pl.ds(s + 4, 64, stride=8), :] = v
        return carry

    lax.fori_loop(0, 4, own_slot, 0)
    lax.fori_loop(0, 4, kept_slot, 0)

    finish(moves)
    take_rows(0)

    @pl.when(lat > 0)
    def _():
        LF[:, pl.ds(0, 24), :] = HL[0]

    @pl.when(lat < n_lat - 1)
    def _():
        LF[:, pl.ds(536, 24), :] = HL[1]

    lane = lax.broadcasted_iota(jnp.int32, (1, 1, half_lon), 2)

    def other(x):
        return jnp.stack([x[1], x[0]])

    def from_east(x):
        turned = pltpu.roll(x, half_lon - 1, 2)
        return jnp.where(lane == half_lon - 1, other(turned), turned)

    def from_west(x):
        turned = pltpu.roll(x, 1, 2)
        return jnp.where(lane == 0, other(turned), turned)

    d, u, v = ND[0], 0.5 * ND[1], 0.5 * ND[2]
    row = lax.broadcasted_iota(jnp.int32, (2, 80, half_lon), 1) - 8 + lat * 64
    on_grid = jnp.logical_and(row >= 0, row < n_lat * 64)
    centre, north, south, east, west = 1.0 - 4.0 * d, d - v, d + v, d - u, d + u
    NF[0] = centre
    NF[1] = north
    NF[2] = south
    NF[3] = east
    NF[4] = west
    NB[0] = centre
    NB[1] = jnp.where(on_grid, pltpu.roll(south, 79, 1), 0.0)
    NB[2] = jnp.where(on_grid, pltpu.roll(north, 1, 1), 0.0)
    NB[3] = from_east(west)
    NB[4] = from_west(east)

    def spread(s, carry):
        for k in range(5):
            CF[k, :, pl.ds(s, 80, stride=8), :] = NF[k]
            CB[k, :, pl.ds(s, 80, stride=8), :] = NB[k]
        return carry

    lax.fori_loop(0, 8, spread, 0)

    def mix(c, mid, up, down):
        return (
            c[0] * mid
            + c[1] * up
            + c[2] * down
            + c[3] * from_east(mid)
            + c[4] * from_west(mid)
        )

    def rows_of(ref, coef, first, r, size):
        f = ref[:, pl.ds(r * 8, (size + 2) * 8), :]
        c = [coef[k, :, pl.ds((first + r) * 8, size * 8), :] for k in range(5)]
        return mix(c, f[:, 8 : 8 + size * 8], f[:, 16:], f[:, : size * 8])

    def over_rows(count, size, body):
        def step(i, carry):
            body(pl.multiple_of(i * size, size), size)
            return carry

        lax.fori_loop(0, count // size, step, 0)
        if count % size:
            body(count - count % size, count % size)

    def sweep3(src, coef, first, dst, count):
        def body(r, size):
            dst[:, pl.ds(r * 8, size * 8), :] = rows_of(src, coef, first, r, size)

        over_rows(count, 8, body)

    slot = lax.broadcasted_iota(jnp.int32, (1, 1, 8, half_lon), 2)

    def cube(x):
        return x.reshape(2, x.shape[1] // 8, 8, half_lon)

    def flat(x):
        return x.reshape(2, x.shape[1] * 8, half_lon)

    def lone(field, coef, at, stride, levels):
        for level in range(levels):
            c = [
                [coef[k, :, pl.ds(at + level + 1 + q, 8, stride=stride), :] for k in range(5)]
                for q in range(len(field) - 2)
            ]
            field = [
                mix(c[q], field[q + 1], field[q + 2], field[q]) for q in range(len(field) - 2)
            ]
        return field

    def forward_part(r, window):
        sweep3(XF, CF, 3, T1, 74)
        sweep3(T1, CF, 4, T2, 72)

        def last(q, size):
            y = rows_of(T2, CF, 5, q, size)
            T1[:, pl.ds(q * 8, size * 8), :] = y
            x = XF[:, pl.ds((q + 3) * 8, size * 8), :]
            jump = jnp.where(slot > 0, cube(x) - pltpu.roll(cube(y), 1, 2), 0.0)
            LF[:, pl.ds(q * 8, size * 8), :] += flat(jump)

        over_rows(70, 8, last)
        before = [E[r, :, pl.ds(2 + q, 8, stride=9), :] for q in range(15)]
        before = lone(before, NF, 2, 9, 3)
        share = jnp.where(tm == 0, 0.0, 1.0) if window == 0 else None
        after = jnp.where(tm == n_tm - 1, 0.0, 1.0)
        for q in range(9):
            jump = XF[:, pl.ds((q + 3) * 8, 8, stride=72), :] - before[q]
            if share is not None:
                jump = share * jump
            LF[:, pl.ds(q * 8, 8, stride=72), :] += jump
            jump = NX[r, :, pl.ds(5 + q, 8, stride=9), :]
            jump = jump - T1[:, pl.ds(q * 8 + 7, 8, stride=72), :]
            NL[window, :, pl.ds(5 + q, 8, stride=9), :] += after * jump

    def backward_part(window):
        sweep3(LF, CB, 6, T1, 68)
        sweep3(T1, CB, 7, T2, 66)

        def last(q, size):
            g = cube(rows_of(T2, CB, 8, q, size))
            g = flat(jnp.where(slot < 7, pltpu.roll(g, 7, 2), 0.0))
            x = XF[:, pl.ds((q + 6) * 8, size * 8), :]
            p = LF[:, pl.ds((q + 3) * 8, size * 8), :]
            w = WF[window, :, pl.ds(q * 8, size * 8), :]
            y = VF[window, :, pl.ds(q * 8, size * 8), :]
            XF[:, pl.ds((q + 6) * 8, size * 8), :] = x - STEP * (w * x - y + p - g)

        over_rows(64, 8, last)
        after = [NL[window, :, pl.ds(5 + q, 8, stride=8), :] for q in range(14)]
        after = lone(after, NB, 5, 8, 3)
        for q in range(8):
            XF[:, pl.ds((q + 6) * 8 + 7, 8, stride=64), :] += STEP * after[q]

    forward_part(0, 0)
    backward_part(0)
    edges(1)
    moves = send_rows(1) + send_before(1) + send_after(1)
    finish(obs_moves)
    lax.fori_loop(0, 4, late_slot, 0)
    finish(moves)
    take_rows(1)
    forward_part(1, 0)

    low = slot < 4

    def pairs(v):
        return v.reshape(2, v.shape[1] // 16, 2, 8, half_lon)

    def pack(src, first, dst, count, size):
        def body(i, carry):
            v = pairs(src[:, pl.ds((first + i * size * 2) * 8, size * 16), :])
            v = jnp.where(low, v[:, :, 0], pltpu.roll(v[:, :, 1], 4, 2))
            dst[:, pl.ds(i * size * 8, size * 8), :] = flat(v)
            return carry

        lax.fori_loop(0, count // size, body, 0)

    def unpack(src, dst, count, size, fill):
        def body(i, carry):
            v = pairs(dst[:, pl.ds(i * size * 16, size * 16), :])
            p = cube(src[:, pl.ds(i * size * 8, size * 8), :])
            out = []
            for half, q in ((v[:, :, 0], pltpu.roll(p, 4, 2)), (v[:, :, 1], p)):
                q = jnp.where(tm == n_tm - 1, fill(half), q)
                out.append(jnp.where(low, pltpu.roll(half, 4, 2), q))
            out = jnp.stack(out, axis=2)
            dst[:, pl.ds(i * size * 16, size * 16), :] = out.reshape(2, size * 16, half_lon)
            return carry

        lax.fori_loop(0, count // size, body, 0)

    pack(LF, 0, PKL, 35, 5)
    SL4[:, pl.ds(5, 70), :] = LF[:, pl.ds(4, 70, stride=8), :]
    early = [Move(PKL, RKL, -1, 0), Move(SL4, NL.at[1], -1, 0)]
    backward_part(0)
    pack(XF, 6, PKX, 32, 4)
    S0[2] = XF[:, pl.ds(52, 64, stride=8), :]
    moves = send_rows(2) + [
        Move(PKX, RKX.at[:, pl.ds(24, 256)], -1, 0),
        Move(PKX.at[:, pl.ds(0, 24)], RKX.at[:, pl.ds(280, 24)], -1, -1),
        Move(PKX.at[:, pl.ds(232, 24)], RKX.at[:, pl.ds(0, 24)], -1, 1),
    ]
    moves += send_after(2)
    finish(early)
    unpack(RKL, LF, 35, 5, jnp.zeros_like)
    finish(moves)
    take_rows(2)
    E[2, :, pl.ds(2, 76), :] = XF[:, pl.ds(3, 76, stride=8), :]
    unpack(RKX, XF, 38, 2, lambda half: jnp.broadcast_to(half[:, :, 7:8], half.shape))

    forward_part(2, 1)
    backward_part(1)
    edges(3)
    moves = send_rows(3) + send_before(3) + send_after(3)

    @pl.when(tm == 0)
    def _():
        E[3] = E[2]

    finish(moves)
    take_rows(3)
    forward_part(3, 1)
    backward_part(1)
    for s in range(8):
        x_out[s] = join(XF[:, pl.ds(48 + s, 64, stride=8), :])
        l_out[s] = join(LF[:, pl.ds(24 + s, 64, stride=8), :])
    assert made[0] == n_transfers


def body(n_tm, n_lat, *arrays):
    states = arrays[0]
    slots, rows, lon = states.shape
    n_obs = arrays[5].shape[-1]
    n_transfers = 44

    def vmem(*shape, kind=F32):
        return pltpu.VMEM(shape, kind)

    shape = jax.ShapeDtypeStruct((slots, rows, lon), F32)
    return pl.pallas_call(
        functools.partial(weave, n_tm, n_lat, n_transfers),
        out_shape=(shape, shape),
        in_specs=[pl.BlockSpec(memory_space=pltpu.VMEM)] * len(arrays),
        out_specs=(pl.BlockSpec(memory_space=pltpu.VMEM),) * 2,
        scratch_shapes=[
            vmem(2, 640, lon // 2),
            vmem(2, 576, lon // 2),
            vmem(2, 592, lon // 2),
            vmem(2, 576, lon // 2),
            vmem(5, 2, 640, lon // 2),
            vmem(5, 2, 640, lon // 2),
            vmem(3, 2, 80, lon // 2),
            vmem(5, 2, 80, lon // 2),
            vmem(5, 2, 80, lon // 2),
            vmem(2, 2, 512, lon // 2),
            vmem(2, 2, 512, lon // 2),
            vmem(4, 2, 2, 48, lon // 2),
            vmem(2, 2, 24, lon // 2),
            vmem(4, 2, 80, lon // 2),
            vmem(4, 2, 80, lon // 2),
            vmem(2, 2, 80, lon // 2),
            vmem(4, 2, 64, lon // 2),
            vmem(4, 2, 64, lon // 2),
            vmem(2, 64, lon // 2),
            vmem(2, 256, lon // 2),
            vmem(2, 280, lon // 2),
            vmem(2, 80, lon // 2),
            vmem(2, 304, lon // 2),
            vmem(2, 280, lon // 2),
            vmem(4, 1, n_obs, kind=jnp.int32),
            vmem(4, 1, n_obs),
            vmem(4, 1, n_obs),
            pltpu.SemaphoreType.DMA((n_transfers,)),
            pltpu.SemaphoreType.DMA((n_transfers,)),
        ],
        compiler_params=pltpu.CompilerParams(
            collective_id=0, has_side_effects=True, vmem_limit_bytes=48 * 1024 * 1024
        ),
    )(*arrays)


def solution(mesh):
    field = P("tm", "lat", None)
    plane = P("lat", None)
    fresh = P(None, "lat", None)
    in_specs = (field, field, plane, plane, plane, field, field, field, fresh, fresh, fresh)
    return jax.shard_map(
        functools.partial(body, mesh.shape["tm"], mesh.shape["lat"]),
        mesh=mesh,
        in_specs=in_specs,
        out_specs=(field, field),
        check_vma=False,
    )
```

profile of v0, /device:TPU:94, one launch (start us, length us, event | category | flops | bytes accessed | tf_op | source)
XLA Modules:
  0.0 83.1 jit_solution(15285439712706199417)
XLA Ops:
  0.6 0.0 copy-start
  0.6 1.0 %copy-done = f32[8,64,256]{2,1,0:T(8,128)S(1)} copy-done((f32[8,64,256]{2,1,0:T(8,128)S(1)}, f32[8,64,256]{2,1,0:T(8,128)}, u32[]{:S(2)}) %copy-start) | copy-done | bytes 524312
  1.7 0.0 copy-start.1
  1.7 1.0 %copy-done.1 = f32[8,64,256]{2,1,0:T(8,128)S(1)} copy-done((f32[8,64,256]{2,1,0:T(8,128)S(1)}, f32[8,64,256]{2,1,0:T(8,128)}, u32[]{:S(2)}) %copy-start.1) | copy-done | bytes 524312
  2.7 0.0 copy-start.2
  2.7 0.8 %copy-done.2 = f32[64,256]{1,0:T(8,128)S(1)} copy-done((f32[64,256]{1,0:T(8,128)S(1)}, f32[64,256]{1,0:T(8,128)}, u32[]{:S(2)}) %copy-start.2) | copy-done | bytes 65560
  3.6 0.0 copy-start.3
  3.6 0.8 %copy-done.3 = f32[64,256]{1,0:T(8,128)S(1)} copy-done((f32[64,256]{1,0:T(8,128)S(1)}, f32[64,256]{1,0:T(8,128)}, u32[]{:S(2)}) %copy-start.3) | copy-done | bytes 65560
  4.4 0.0 copy-start.4
  4.4 0.8 %copy-done.4 = f32[64,256]{1,0:T(8,128)S(1)} copy-done((f32[64,256]{1,0:T(8,128)S(1)}, f32[64,256]{1,0:T(8,128)}, u32[]{:S(2)}) %copy-start.4) | copy-done | bytes 65560
  5.2 0.0 copy-start.5
  5.2 0.8 copy-done.5
  6.0 0.0 copy-start.6
  6.0 0.8 copy-done.6
  6.8 0.0 copy-start.7
  6.8 0.8 copy-done.7
  7.5 0.0 copy-start.8
  7.5 0.7 copy-done.8
  8.2 0.0 copy-start.9
  8.2 0.7 copy-done.9
  8.9 0.0 copy-start.10
  9.0 0.7 copy-done.10
  9.7 71.8 %shard_map.122 = (f32[8,64,256]{2,1,0:T(8,128)S(1)}, f32[8,64,256]{2,1,0:T(8,128)S(1)}) custom-call(f32[8,64,256]{2,1,0:T(8,128)S(1)} %copy-done, f32[8,64,256]{2,1,0:T(8,128)S(1)} %copy-done.1, f32[64,256]{1,0:T(8,128)S(1)} %copy-done.2, f32[64,256]{1,0:T(8,128)S(1)} %copy-done.3, f32[64,256]{1,0:T(8,128)S(1)} %copy-done.4, s32[8,1,1024]{2,1,0:T(1,128)S(1)} %copy-done.5, ...), custom_call_target="tpu_custom_call" | custom-call | tf_op jit(solution)/shard_map/pallas_call | solution.py:506
  81.5 0.8 copy.15
  82.3 0.8 copy.16
Async XLA Ops:
  0.6 1.0 %copy-start = (f32[8,64,256]{2,1,0:T(8,128)S(1)}, f32[8,64,256]{2,1,0:T(8,128)}, u32[]{:S(2)}) copy-start(f32[8,64,256]{2,1,0:T(8,128)} %refs_0_.1) | copy-start | bytes 1572868
  1.7 1.0 %copy-start.1 = (f32[8,64,256]{2,1,0:T(8,128)S(1)}, f32[8,64,256]{2,1,0:T(8,128)}, u32[]{:S(2)}) copy-start(f32[8,64,256]{2,1,0:T(8,128)} %refs_1_.1) | copy-start | bytes 1572868
  2.7 0.8 %copy-start.2 = (f32[64,256]{1,0:T(8,128)S(1)}, f32[64,256]{1,0:T(8,128)}, u32[]{:S(2)}) copy-start(f32[64,256]{1,0:T(8,128)} %refs_2_.1) | copy-start | bytes 196612
  3.6 0.8 %copy-start.3 = (f32[64,256]{1,0:T(8,128)S(1)}, f32[64,256]{1,0:T(8,128)}, u32[]{:S(2)}) copy-start(f32[64,256]{1,0:T(8,128)} %refs_3_.1) | copy-start | bytes 196612
  4.4 0.8 %copy-start.4 = (f32[64,256]{1,0:T(8,128)S(1)}, f32[64,256]{1,0:T(8,128)}, u32[]{:S(2)}) copy-start(f32[64,256]{1,0:T(8,128)} %refs_4_.1) | copy-start | bytes 196612
  5.2 0.8 copy-start.5
  6.0 0.8 copy-start.6
  6.8 0.8 copy-start.7
  7.5 0.7 copy-start.8
  8.2 0.7 copy-start.9
  8.9 0.7 copy-start.10
where the time goes:
time: 83.8 us; the launch traced here: 83.1 us
  Pallas kernels  71.8 us (86%)
  local copies, waits for them, and re-layouts  10.6 us (13%)
    pallas_call x1, Pallas kernels, body(): pl.pallas_call(functools.partial(weave, n_tm, n_lat, n_transfers), out_sh...  71.8 us
    unnamed x24, local copies, waits for them, and re-layouts  10.6 us

commit v1 on v0

v1 whole, which is shorter than its diff:
```python
import functools

import jax
import jax.numpy as jnp
from jax import lax
from jax.experimental import pallas as pl
from jax.experimental.pallas import tpu as pltpu
from jax.sharding import PartitionSpec as P

MESH = pl.DeviceIdType.MESH
STEP = 0.15
F32 = jnp.float32


def weave(n_tm, n_lat, n_transfers, *refs):
    (
        states_hbm,
        mults_hbm,
        diff_hbm,
        zonal_hbm,
        merid_hbm,
        cells_hbm,
        values_hbm,
        weights_hbm,
        f_cells_hbm,
        f_values_hbm,
        f_weights_hbm,
        x_out,
        l_out,
        XF,
        LF,
        T1,
        T2,
        Y,
        U1,
        U2,
        CF,
        CB,
        ND,
        NF,
        NB,
        WF,
        VF,
        HX,
        HL,
        E,
        NX,
        NL,
        S7,
        S0,
        SL0,
        PKX,
        PKL,
        SL4,
        RKX,
        RKL,
        states,
        mults,
        speeds,
        cells,
        values,
        weights,
        ssem,
        rsem,
        lsem,
    ) = refs
    lon = 2 * XF.shape[-1]
    half_lon = lon // 2
    tm = lax.axis_index("tm")
    lat = lax.axis_index("lat")
    made = [0]

    def inside(dt, dl):
        ok = True
        if dt > 0:
            ok = tm < n_tm - 1
        elif dt < 0:
            ok = tm > 0
        if dl > 0:
            ok = jnp.logical_and(ok, lat < n_lat - 1)
        elif dl < 0:
            ok = jnp.logical_and(ok, lat > 0)
        return ok

    class Move:
        def __init__(self, src, dst, dt, dl):
            i = made[0]
            made[0] += 1
            assert i < n_transfers
            self.to, self.by = inside(dt, dl), inside(-dt, -dl)
            self.copy = pltpu.make_async_remote_copy(
                src_ref=src,
                dst_ref=dst,
                send_sem=ssem.at[i],
                recv_sem=rsem.at[i],
                device_id=(tm + dt, lat + dl),
                device_id_type=MESH,
            )
            pl.when(self.to)(self.copy.start)

        def sent(self):
            pl.when(self.to)(self.copy.wait_send)
            self.to = None

        def finish(self):
            if self.to is not None:
                self.sent()
            pl.when(self.by)(self.copy.wait_recv)

    fetched = [
        pltpu.make_async_copy(src, dst, lsem.at[i])
        for i, (src, dst) in enumerate(
            (
                (states_hbm, states),
                (mults_hbm, mults),
                (diff_hbm, speeds.at[0]),
                (zonal_hbm, speeds.at[1]),
                (merid_hbm, speeds.at[2]),
                (cells_hbm, cells.at[pl.ds(0, 8)]),
                (values_hbm, values.at[pl.ds(0, 8)]),
                (weights_hbm, weights.at[pl.ds(0, 8)]),
            )
        )
    ]
    for copy in fetched:
        copy.start()
    fresh = [
        pltpu.make_async_copy(src, dst.at[pl.ds(8, 4)], lsem.at[8 + i])
        for i, (src, dst) in enumerate(
            ((f_cells_hbm, cells), (f_values_hbm, values), (f_weights_hbm, weights))
        )
    ]

    @pl.when(tm == n_tm - 1)
    def _():
        for copy in fresh:
            copy.start()

    barrier = pltpu.get_barrier_semaphore()
    greeted = 0
    for dt in (-1, 0, 1):
        for dl in (-1, 0, 1):
            if dt == 0 and dl == 0:
                continue
            ok = inside(dt, dl)

            @pl.when(ok)
            def _():
                pl.semaphore_signal(
                    barrier, inc=1, device_id=(tm + dt, lat + dl), device_id_type=MESH
                )

            greeted = greeted + ok.astype(jnp.int32)

    whole = slice(None)

    def blank(ref, *at):
        ref[at] = jnp.zeros(ref.at[at].shape, ref.dtype)

    @pl.when(lat == 0)
    def _():
        for r in range(4):
            blank(E, r, whole, slice(0, 8))
            blank(NX, r, whole, slice(0, 8))
        for k in range(3):
            blank(ND, k, whole, slice(0, 8))
        blank(NL, 0, whole, slice(0, 8))
        blank(XF, whole, slice(0, 48))
        blank(LF, whole, slice(0, 24))
        blank(RKX, whole, slice(0, 24))

    @pl.when(lat == n_lat - 1)
    def _():
        for r in range(4):
            blank(E, r, whole, slice(72, 80))
            blank(NX, r, whole, slice(72, 80))
        for k in range(3):
            blank(ND, k, whole, slice(72, 80))
        blank(NL, 0, whole, slice(72, 80))
        blank(XF, whole, slice(560, 608))
        blank(LF, whole, slice(536, 560))
        blank(RKX, whole, slice(280, 304))

    @pl.when(tm == 0)
    def _():
        blank(E, 0)
        blank(E, 1)

    @pl.when(tm == n_tm - 1)
    def _():
        for r in range(4):
            blank(NX, r)
        blank(NL, 0)
        blank(NL, 1)

    blank(XF, whole, slice(608, 640))
    blank(E, 2, whole, slice(72, 80))
    blank(LF, whole, slice(560, 576))

    def split(x):
        return jnp.stack([x[:, :half_lon], x[:, half_lon:]])

    def join(x):
        return jnp.concatenate([x[0], x[1]], axis=1)

    for copy in fetched[:5]:
        copy.wait()
    for s in range(8):
        XF[:, pl.ds(48 + s, 64, stride=8), :] = split(states[s])
        LF[:, pl.ds(24 + s, 64, stride=8), :] = split(mults[s])
    S7[0] = split(states[7])
    S0[0] = split(states[0])
    SL0[...] = split(mults[0])
    for k in range(3):
        ND[k, :, pl.ds(8, 64), :] = split(speeds[k])

    pl.semaphore_wait(barrier, greeted)

    def send_corners(r, before=True):
        moves = []
        if before:
            moves += [
                Move(S7.at[r, :, pl.ds(0, 8)], E.at[r, :, pl.ds(72, 8)], 1, -1),
                Move(S7.at[r, :, pl.ds(56, 8)], E.at[r, :, pl.ds(0, 8)], 1, 1),
            ]
        return moves + [
            Move(S0.at[r, :, pl.ds(0, 8)], NX.at[r, :, pl.ds(72, 8)], -1, -1),
            Move(S0.at[r, :, pl.ds(56, 8)], NX.at[r, :, pl.ds(0, 8)], -1, 1),
        ]

    def send_slots(r, before=True):
        moves = [Move(S7.at[r], E.at[r, :, pl.ds(8, 64)], 1, 0)] if before else []
        return moves + [Move(S0.at[r], NX.at[r, :, pl.ds(8, 64)], -1, 0)]

    def send_rows(r):
        return [
            Move(XF.at[:, pl.ds(48, 48)], HX.at[r, 1], 0, -1),
            Move(XF.at[:, pl.ds(512, 48)], HX.at[r, 0], 0, 1),
        ]

    def finish(moves):
        for move in moves:
            move.finish()

    def take_rows(r):
        @pl.when(lat > 0)
        def _():
            XF[:, pl.ds(0, 48), :] = HX[r, 0]

        @pl.when(lat < n_lat - 1)
        def _():
            XF[:, pl.ds(560, 48), :] = HX[r, 1]

    def edges(r):
        S7[r] = XF[:, pl.ds(55, 64, stride=8), :]
        S0[r] = XF[:, pl.ds(48, 64, stride=8), :]

    slot_moves = send_corners(0) + [
        Move(SL0.at[:, pl.ds(0, 8)], NL.at[0, :, pl.ds(72, 8)], -1, -1),
        Move(SL0.at[:, pl.ds(56, 8)], NL.at[0, :, pl.ds(0, 8)], -1, 1),
    ]
    row_moves = send_rows(0)
    row_moves += [
        Move(LF.at[:, pl.ds(24, 24)], HL.at[1], 0, -1),
        Move(LF.at[:, pl.ds(512, 24)], HL.at[0], 0, 1),
        Move(ND.at[:, :, pl.ds(8, 8)], ND.at[:, :, pl.ds(72, 8)], 0, -1),
        Move(ND.at[:, :, pl.ds(64, 8)], ND.at[:, :, pl.ds(0, 8)], 0, 1),
    ]
    slot_moves += send_slots(0) + [Move(SL0, NL.at[0, :, pl.ds(8, 64)], -1, 0)]
    for copy in fetched[5:]:
        copy.wait()
    obs_moves = [
        Move(cells.at[pl.ds(0, 4)], cells.at[pl.ds(8, 4)], -1, 0),
        Move(values.at[pl.ds(0, 4)], values.at[pl.ds(8, 4)], -1, 0),
        Move(weights.at[pl.ds(0, 4)], weights.at[pl.ds(8, 4)], -1, 0),
    ]

    n_obs = cells.shape[-1]

    def tables(c, y, w):
        row = lax.shift_right_logical(c, 8)
        column = lax.bitwise_and(c, 255)
        on_row = lax.broadcasted_iota(jnp.int32, (64, n_obs), 0) == row
        on_column = lax.broadcasted_iota(jnp.int32, (lon, n_obs), 0) == column
        wy = w * y
        parts = []
        for full in (w, wy):
            high = full.astype(jnp.bfloat16).astype(F32)
            for part in (high, full - high):
                parts.append(jnp.where(on_row, part, 0.0).astype(jnp.bfloat16))
        left = jnp.concatenate(parts, axis=0)
        right = jnp.where(on_column, 1.0, 0.0).astype(jnp.bfloat16)
        out = lax.dot_general(
            left, right, (((1,), (1,)), ((), ())), preferred_element_type=F32
        )
        return split(out[0:64] + out[64:128]), split(out[128:192] + out[192:256])

    def own_slot(s, carry):
        w, v = tables(cells[s], values[s], weights[s])
        WF[0, :, pl.ds(s, 64, stride=8), :] = w
        VF[0, :, pl.ds(s, 64, stride=8), :] = v
        return carry

    def kept_slot(s, carry):
        w, v = tables(cells[s + 4], values[s + 4], weights[s + 4])
        WF[0, :, pl.ds(s + 4, 64, stride=8), :] = w
        VF[0, :, pl.ds(s + 4, 64, stride=8), :] = v
        WF[1, :, pl.ds(s, 64, stride=8), :] = w
        VF[1, :, pl.ds(s, 64, stride=8), :] = v
        return carry

    def late_slot(s, carry):
        w, v = tables(cells[s + 8], values[s + 8], weights[s + 8])
        WF[1, :, pl.ds(s + 4, 64, stride=8), :] = w
        VF[1, :, pl.ds(s + 4, 64, stride=8), :] = v
        return carry

    lane = lax.broadcasted_iota(jnp.int32, (1, 1, half_lon), 2)

    def other(x):
        return jnp.stack([x[1], x[0]])

    def from_east(x):
        turned = pltpu.roll(x, half_lon - 1, 2)
        return jnp.where(lane == half_lon - 1, other(turned), turned)

    def from_west(x):
        turned = pltpu.roll(x, 1, 2)
        return jnp.where(lane == 0, other(turned), turned)

    def combine(first, count, kept):
        rows = pl.ds(first, count)
        d, u, v = ND[0, :, rows, :], 0.5 * ND[1, :, rows, :], 0.5 * ND[2, :, rows, :]
        row = lax.broadcasted_iota(jnp.int32, (2, count, half_lon), 1) + (first - 8) + lat * 64
        on_grid = jnp.logical_and(row >= 0, row < n_lat * 64)
        centre, north, south, east, west = 1.0 - 4.0 * d, d - v, d + v, d - u, d + u
        here = pl.ds(first + kept.start, kept.stop - kept.start)
        for k, value in enumerate((centre, north, south, east, west)):
            NF[k, :, here, :] = value[:, kept]
        adjoint = (
            centre,
            jnp.where(on_grid, pltpu.roll(south, count - 1, 1), 0.0),
            jnp.where(on_grid, pltpu.roll(north, 1, 1), 0.0),
            from_east(west),
            from_west(east),
        )
        for k, value in enumerate(adjoint):
            NB[k, :, here, :] = value[:, kept]

    def spread(first, count):
        def body(s, carry):
            for k in range(5):
                at = pl.ds(first * 8 + s, count, stride=8)
                CF[k, :, at, :] = NF[k, :, pl.ds(first, count), :]
                CB[k, :, at, :] = NB[k, :, pl.ds(first, count), :]
            return carry

        lax.fori_loop(0, 8, body, 0)

    def mix(c, mid, up, down):
        return (
            c[0] * mid
            + c[1] * up
            + c[2] * down
            + c[3] * from_east(mid)
            + c[4] * from_west(mid)
        )

    def tile(row, off):
        return pl.ds((row + off) * 8, 8)

    def one(src, off, coef, row):
        f = [src[:, tile(row + j, off), :] for j in (-1, 0, 1)]
        c = [coef[k, :, tile(row, 8), :] for k in range(5)]
        return mix(c, f[1], f[2], f[0])

    def over(rows, work):
        calc, store = work
        done = [calc(row) for row in rows]
        for row, value in zip(rows, done):
            store(row, value)

    def between(low, high, work):
        size = (high - low) // 2

        def step(i, carry):
            over([low + i * size + q for q in range(size)], work)
            return carry

        lax.fori_loop(0, 2, step, 0)

    def substep(src, off, coef, dst, dst_off):
        def store(row, value):
            dst[:, tile(row, dst_off), :] = value

        return (lambda row: one(src, off, coef, row)), store

    slot = lax.broadcasted_iota(jnp.int32, (1, 8, half_lon), 1)

    def cube(x):
        return x.reshape(2, x.shape[1] // 8, 8, half_lon)

    def flat(x):
        return x.reshape(2, x.shape[1] * 8, half_lon)

    def lone(field, coef, at, stride, levels):
        for level in range(levels):
            c = [
                [coef[k, :, pl.ds(at + level + 1 + q, 8, stride=stride), :] for k in range(5)]
                for q in range(len(field) - 2)
            ]
            field = [
                mix(c[q], field[q + 1], field[q + 2], field[q]) for q in range(len(field) - 2)
            ]
        return field

    def works(window):
        share = jnp.where(tm == 0, 0.0, 1.0) if window == 0 else 1.0

        def calc_jump(row):
            y = one(T2, 4, CF, row)
            x = XF[:, tile(row, 6), :]
            jump = jnp.where(slot > 0, x - pltpu.roll(y, 1, 1), share * x)
            return y, LF[:, tile(row, 3), :] + jump

        def store_jump(row, value):
            Y[:, tile(row, 3), :] = value[0]
            LF[:, tile(row, 3), :] = value[1]

        def calc_state(row):
            g = one(U2, 1, CB, row)
            g = jnp.where(slot < 7, pltpu.roll(g, 7, 1), 0.0)
            x = XF[:, tile(row, 6), :]
            p = LF[:, tile(row, 3), :]
            w = WF[window, :, tile(row, 0), :]
            y = VF[window, :, tile(row, 0), :]
            return x - STEP * (w * x - y + p - g)

        def store_state(row, value):
            XF[:, tile(row, 6), :] = value

        return (
            substep(XF, 6, CF, T1, 5),
            substep(T1, 5, CF, T2, 4),
            (calc_jump, store_jump),
            substep(LF, 3, CB, U1, 2),
            substep(U1, 2, CB, U2, 1),
            (calc_state, store_state),
        )

    def interior(window):
        for i, work in enumerate(works(window)):
            between(1 + i, 63 - i, work)

    def ends(window):
        for i, work in enumerate(works(window)):
            over([row for row in range(i - 5, i + 1)] + [row for row in range(63 - i, 69 - i)], work)

    def slots_beside(r, window):
        before = [E[r, :, pl.ds(2 + q, 8, stride=9), :] for q in range(15)]
        before = lone(before, NF, 2, 9, 3)
        after_on = jnp.where(tm == n_tm - 1, 0.0, 1.0)
        for q in range(9):
            jump = NX[r, :, pl.ds(5 + q, 8, stride=9), :]
            jump = jump - Y[:, pl.ds(q * 8 + 7, 8, stride=72), :]
            NL[window, :, pl.ds(5 + q, 8, stride=9), :] += after_on * jump
        after = [NL[window, :, pl.ds(5 + q, 8, stride=8), :] for q in range(14)]
        after = lone(after, NB, 5, 8, 3)
        for q in range(9):
            first = before[q]
            if window == 0:
                first = jnp.where(tm == 0, 0.0, 1.0) * first
            LF[:, pl.ds(q * 8, 8, stride=72), :] -= first
            XF[:, pl.ds((q + 3) * 8, 8, stride=72), :] += STEP * first
        for q in range(8):
            XF[:, pl.ds((q + 6) * 8 + 7, 8, stride=64), :] += STEP * after[q]

    combine(8, 64, slice(0, 64))
    spread(8, 64)
    lax.fori_loop(0, 4, own_slot, 0)
    lax.fori_loop(0, 4, kept_slot, 0)
    interior(0)
    finish(row_moves)
    take_rows(0)

    @pl.when(lat > 0)
    def _():
        LF[:, pl.ds(0, 24), :] = HL[0]

    @pl.when(lat < n_lat - 1)
    def _():
        LF[:, pl.ds(536, 24), :] = HL[1]

    combine(0, 24, slice(0, 16))
    combine(56, 24, slice(8, 24))
    spread(0, 16)
    spread(64, 16)
    ends(0)
    finish(slot_moves)
    slots_beside(0, 0)
    edges(1)
    slot_moves = send_corners(1)
    row_moves = send_rows(1)
    slot_moves += send_slots(1)
    interior(0)
    finish(obs_moves)

    @pl.when(tm == n_tm - 1)
    def _():
        for copy in fresh:
            copy.wait()

    lax.fori_loop(0, 4, late_slot, 0)
    finish(row_moves)
    take_rows(1)
    ends(0)
    finish(slot_moves)
    slots_beside(1, 0)

    low = lax.broadcasted_iota(jnp.int32, (1, 1, 8, half_lon), 2) < 4

    def pairs(v):
        return v.reshape(2, v.shape[1] // 16, 2, 8, half_lon)

    def pack(src, first, dst, count, size):
        def body(i, carry):
            v = pairs(src[:, pl.ds((first + i * size * 2) * 8, size * 16), :])
            v = jnp.where(low, v[:, :, 0], pltpu.roll(v[:, :, 1], 4, 2))
            dst[:, pl.ds(i * size * 8, size * 8), :] = flat(v)
            return carry

        lax.fori_loop(0, count // size, body, 0)

    def unpack(src, dst, first, count, size, fill):
        def body(i, carry):
            at = first + i * size
            v = pairs(dst[:, pl.ds(at * 16, size * 16), :])
            p = cube(src[:, pl.ds(at * 8, size * 8), :])
            out = []
            for half, q in ((v[:, :, 0], pltpu.roll(p, 4, 2)), (v[:, :, 1], p)):
                q = jnp.where(tm == n_tm - 1, fill(half), q)
                out.append(jnp.where(low, pltpu.roll(half, 4, 2), q))
            out = jnp.stack(out, axis=2)
            dst[:, pl.ds(at * 16, size * 16), :] = out.reshape(2, size * 16, half_lon)
            return carry

        lax.fori_loop(0, count // size, body, 0)

    pack(LF, 0, PKL, 35, 5)
    SL4[:, pl.ds(5, 70), :] = LF[:, pl.ds(4, 70, stride=8), :]
    early = [Move(PKL, RKL, -1, 0), Move(SL4, NL.at[1], -1, 0)]
    pack(XF, 6, PKX, 32, 4)
    S0[2] = XF[:, pl.ds(52, 64, stride=8), :]
    slot_moves = send_corners(2, before=False)
    corner_moves = [
        Move(PKX.at[:, pl.ds(0, 24)], RKX.at[:, pl.ds(280, 24)], -1, -1),
        Move(PKX.at[:, pl.ds(232, 24)], RKX.at[:, pl.ds(0, 24)], -1, 1),
    ]
    row_moves = send_rows(2)
    slab_moves = [Move(PKX, RKX.at[:, pl.ds(24, 256)], -1, 0)]
    slot_moves += send_slots(2, before=False)
    E[2, :, pl.ds(8, 64), :] = XF[:, pl.ds(51, 64, stride=8), :]

    def repeat(half):
        return jnp.broadcast_to(half[:, :, 7:8], half.shape)

    finish(early)
    unpack(RKL, LF, 0, 35, 5, jnp.zeros_like)
    finish(slab_moves)
    for move in row_moves:
        move.sent()
    unpack(RKX, XF, 3, 32, 8, repeat)

    interior(1)
    finish(row_moves)
    take_rows(2)
    E[2, :, pl.ds(2, 6), :] = XF[:, pl.ds(3, 6, stride=8), :]
    E[2, :, pl.ds(72, 6), :] = XF[:, pl.ds(563, 6, stride=8), :]
    finish(corner_moves)
    unpack(RKX, XF, 0, 3, 3, repeat)
    unpack(RKX, XF, 35, 3, 3, repeat)
    ends(1)
    finish(slot_moves)
    slots_beside(2, 1)
    edges(3)
    slot_moves = send_corners(3)
    row_moves = send_rows(3)
    slot_moves += send_slots(3)

    @pl.when(tm == 0)
    def _():
        E[3] = E[2]

    interior(1)
    finish(row_moves)
    take_rows(3)
    ends(1)
    finish(slot_moves)
    slots_beside(3, 1)
    results = [
        pltpu.make_async_copy(XF.at[:, pl.ds(48, 512)], x_out, lsem.at[0]),
        pltpu.make_async_copy(LF.at[:, pl.ds(24, 512)], l_out, lsem.at[1]),
    ]
    for copy in results:
        copy.start()
    for copy in results:
        copy.wait()
    assert made[0] == n_transfers


def unweave(x_hbm, l_hbm, x_out, l_out, x_ref, l_ref, sems):
    copies = [
        pltpu.make_async_copy(src, dst, sems.at[i])
        for i, (src, dst) in enumerate(((x_hbm, x_ref), (l_hbm, l_ref)))
    ]
    for copy in copies:
        copy.start()
    for copy, ref, out in zip(copies, (x_ref, l_ref), (x_out, l_out)):
        copy.wait()
        for s in range(8):
            x = ref[:, pl.ds(s, 64, stride=8), :]
            out[s] = jnp.concatenate([x[0], x[1]], axis=1)


def body(n_tm, n_lat, *arrays):
    states = arrays[0]
    slots, rows, lon = states.shape
    n_obs = arrays[5].shape[-1]
    n_transfers = 44

    def vmem(*shape, kind=F32):
        return pltpu.VMEM(shape, kind)

    woven = jax.ShapeDtypeStruct((2, slots * rows, lon // 2), F32)
    shape = jax.ShapeDtypeStruct((slots, rows, lon), F32)
    fields = pl.pallas_call(
        functools.partial(weave, n_tm, n_lat, n_transfers),
        out_shape=(woven, woven),
        in_specs=[pl.BlockSpec(memory_space=pltpu.HBM)] * len(arrays),
        out_specs=(pl.BlockSpec(memory_space=pltpu.HBM),) * 2,
        scratch_shapes=[
            vmem(2, 640, lon // 2),
            vmem(2, 576, lon // 2),
            vmem(2, 592, lon // 2),
            vmem(2, 576, lon // 2),
            vmem(2, 576, lon // 2),
            vmem(2, 544, lon // 2),
            vmem(2, 528, lon // 2),
            vmem(5, 2, 640, lon // 2),
            vmem(5, 2, 640, lon // 2),
            vmem(3, 2, 80, lon // 2),
            vmem(5, 2, 80, lon // 2),
            vmem(5, 2, 80, lon // 2),
            vmem(2, 2, 512, lon // 2),
            vmem(2, 2, 512, lon // 2),
            vmem(4, 2, 2, 48, lon // 2),
            vmem(2, 2, 24, lon // 2),
            vmem(4, 2, 80, lon // 2),
            vmem(4, 2, 80, lon // 2),
            vmem(2, 2, 80, lon // 2),
            vmem(4, 2, 64, lon // 2),
            vmem(4, 2, 64, lon // 2),
            vmem(2, 64, lon // 2),
            vmem(2, 256, lon // 2),
            vmem(2, 280, lon // 2),
            vmem(2, 80, lon // 2),
            vmem(2, 304, lon // 2),
            vmem(2, 280, lon // 2),
            vmem(slots, rows, lon),
            vmem(slots, rows, lon),
            vmem(3, rows, lon),
            vmem(12, 1, n_obs, kind=jnp.int32),
            vmem(12, 1, n_obs),
            vmem(12, 1, n_obs),
            pltpu.SemaphoreType.DMA((n_transfers,)),
            pltpu.SemaphoreType.DMA((n_transfers,)),
            pltpu.SemaphoreType.DMA((11,)),
        ],
        compiler_params=pltpu.CompilerParams(
            collective_id=0, has_side_effects=True, vmem_limit_bytes=64 * 1024 * 1024 - 65536
        ),
    )(*arrays)
    return pl.pallas_call(
        unweave,
        out_shape=(shape, shape),
        in_specs=[pl.BlockSpec(memory_space=pltpu.HBM)] * 2,
        out_specs=(pl.BlockSpec(memory_space=pltpu.VMEM),) * 2,
        scratch_shapes=[
            vmem(2, 512, lon // 2),
            vmem(2, 512, lon // 2),
            pltpu.SemaphoreType.DMA((2,)),
        ],
        compiler_params=pltpu.CompilerParams(vmem_limit_bytes=64 * 1024 * 1024 - 65536),
    )(*fields)


def solution(mesh):
    field = P("tm", "lat", None)
    plane = P("lat", None)
    fresh = P(None, "lat", None)
    in_specs = (field, field, plane, plane, plane, field, field, field, fresh, fresh, fresh)
    return jax.shard_map(
        functools.partial(body, mesh.shape["tm"], mesh.shape["lat"]),
        mesh=mesh,
        in_specs=in_specs,
        out_specs=(field, field),
        check_vma=False,
    )
```

time: 83.8 us -> 50 us (0.60)
  the two profiles are of different devices: /device:TPU:94 before, /device:TPU:93 now
where the time goes in v1:
time: 50 us; the launch traced here: 49.8 us
  Pallas kernels  49.2 us (98%)
  between operations  0.64 us (1%)
    pallas_call x1, Pallas kernels, body(): pl.pallas_call(functools.partial(weave, n_tm, n_lat, n_transfers), out_sh...  47 us
    pallas_call x1, Pallas kernels, body(): pl.pallas_call(unweave, out_shape=(shape, shape), in_specs=[pl.BlockSpec(...  2.19 us

profile of v1, /device:TPU:93, one launch (start us, length us, event | category | flops | bytes accessed | tf_op | source)
XLA Modules:
  0.0 49.8 jit_solution(10413014333335153128)
XLA Ops:
  0.6 47.0 %shard_map.122 = (f32[2,512,128]{2,1,0:T(8,128)}, f32[2,512,128]{2,1,0:T(8,128)}) custom-call(f32[8,64,256]{2,1,0:T(8,128)} %refs_0_.1, f32[8,64,256]{2,1,0:T(8,128)} %refs_1_.1, f32[64,256]{1,0:T(8,128)} %refs_2_.1, f32[64,256]{1,0:T(8,128)} %refs_3_.1, f32[64,256]{1,0:T(8,128)} %refs_4_.1, s32[8,1,1024]{2,1,0:T(1,128)} %refs_5_.1, f32[8,1,1024]{2,1,0:T(1,128)} %refs_6_.1, ...), custom_call_target="tpu_custom_call" | custom-call | tf_op jit(solution)/shard_map/pallas_call | solution.py:636
  47.6 2.2 %shard_map.123 = (f32[8,64,256]{2,1,0:T(8,128)}, f32[8,64,256]{2,1,0:T(8,128)}) custom-call(f32[2,512,128]{2,1,0:T(8,128)} %get-tuple-element.4.x_hbm, f32[2,512,128]{2,1,0:T(8,128)} %get-tuple-element.5.l_hbm), custom_call_target="tpu_custom_call" | custom-call | tf_op jit(solution)/shard_map/pallas_call | solution.py:683

commit v2 on v1

--- a/solution.py
+++ b/solution.py
@@ -54,6 +54,10 @@
         SL4,
         RKX,
         RKL,
+        SXZ,
+        SLZ,
+        RXZ,
+        RLZ,
         states,
         mults,
         speeds,
@@ -475,6 +479,35 @@
         for q in range(8):
             XF[:, pl.ds((q + 6) * 8 + 7, 8, stride=64), :] += STEP * after[q]
 
+    low = lax.broadcasted_iota(jnp.int32, (1, 1, 8, half_lon), 2) < 4
+
+    def pairs(v):
+        return v.reshape(2, v.shape[1] // 16, 2, 8, half_lon)
+
+    def pack(src, first, dst, at, count, size):
+        def body(i, carry):
+            v = pairs(src[:, pl.ds((first + i * size * 2) * 8, size * 16), :])
+            v = jnp.where(low, v[:, :, 0], pltpu.roll(v[:, :, 1], 4, 2))
+            dst[:, pl.ds((at + i * size) * 8, size * 8), :] = flat(v)
+            return carry
+
+        lax.fori_loop(0, count // size, body, 0)
+
+    def unpack(src, dst, first, count, size, fill):
+        def body(i, carry):
+            at = first + i * size
+            v = pairs(dst[:, pl.ds(at * 16, size * 16), :])
+            p = cube(src[:, pl.ds(at * 8, size * 8), :])
+            out = []
+            for half, q in ((v[:, :, 0], pltpu.roll(p, 4, 2)), (v[:, :, 1], p)):
+                q = jnp.where(tm == n_tm - 1, fill(half), q)
+                out.append(jnp.where(low, pltpu.roll(half, 4, 2), q))
+            out = jnp.stack(out, axis=2)
+            dst[:, pl.ds(at * 16, size * 16), :] = out.reshape(2, size * 16, half_lon)
+            return carry
+
+        lax.fori_loop(0, count // size, body, 0)
+
     combine(8, 64, slice(0, 64))
     spread(8, 64)
     lax.fori_loop(0, 4, own_slot, 0)
@@ -503,6 +536,12 @@
     row_moves = send_rows(1)
     slot_moves += send_slots(1)
     interior(0)
+    pack(XF, 12, PKX, 3, 26, 13)
+    pack(LF, 6, PKL, 3, 29, 29)
+    early = [
+        Move(PKX.at[:, pl.ds(24, 208)], RKX.at[:, pl.ds(48, 208)], -1, 0),
+        Move(PKL.at[:, pl.ds(24, 232)], RKL.at[:, pl.ds(24, 232)], -1, 0),
+    ]
     finish(obs_moves)
 
     @pl.when(tm == n_tm - 1)
@@ -511,76 +550,63 @@
             copy.wait()
 
     lax.fori_loop(0, 4, late_slot, 0)
+    finish(slot_moves)
     finish(row_moves)
     take_rows(1)
     ends(0)
-    finish(slot_moves)
     slots_beside(1, 0)
 
-    low = lax.broadcasted_iota(jnp.int32, (1, 1, 8, half_lon), 2) < 4
-
-    def pairs(v):
-        return v.reshape(2, v.shape[1] // 16, 2, 8, half_lon)
-
-    def pack(src, first, dst, count, size):
-        def body(i, carry):
-            v = pairs(src[:, pl.ds((first + i * size * 2) * 8, size * 16), :])
-            v = jnp.where(low, v[:, :, 0], pltpu.roll(v[:, :, 1], 4, 2))
-            dst[:, pl.ds(i * size * 8, size * 8), :] = flat(v)
-            return carry
-
-        lax.fori_loop(0, count // size, body, 0)
-
-    def unpack(src, dst, first, count, size, fill):
-        def body(i, carry):
-            at = first + i * size
-            v = pairs(dst[:, pl.ds(at * 16, size * 16), :])
-            p = cube(src[:, pl.ds(at * 8, size * 8), :])
-            out = []
-            for half, q in ((v[:, :, 0], pltpu.roll(p, 4, 2)), (v[:, :, 1], p)):
-                q = jnp.where(tm == n_tm - 1, fill(half), q)
-                out.append(jnp.where(low, pltpu.roll(half, 4, 2), q))
-            out = jnp.stack(out, axis=2)
-            dst[:, pl.ds(at * 16, size * 16), :] = out.reshape(2, size * 16, half_lon)
-            return carry
-
-        lax.fori_loop(0, count // size, body, 0)
-
-    pack(LF, 0, PKL, 35, 5)
-    SL4[:, pl.ds(5, 70), :] = LF[:, pl.ds(4, 70, stride=8), :]
-    early = [Move(PKL, RKL, -1, 0), Move(SL4, NL.at[1], -1, 0)]
-    pack(XF, 6, PKX, 32, 4)
+    row_moves = send_rows(2)
+    pack(XF, 6, PKX, 0, 3, 3)
+    pack(XF, 64, PKX, 29, 3, 3)
     S0[2] = XF[:, pl.ds(52, 64, stride=8), :]
     slot_moves = send_corners(2, before=False)
     corner_moves = [
         Move(PKX.at[:, pl.ds(0, 24)], RKX.at[:, pl.ds(280, 24)], -1, -1),
         Move(PKX.at[:, pl.ds(232, 24)], RKX.at[:, pl.ds(0, 24)], -1, 1),
     ]
-    row_moves = send_rows(2)
-    slab_moves = [Move(PKX, RKX.at[:, pl.ds(24, 256)], -1, 0)]
+    pack(LF, 0, PKL, 0, 3, 3)
+    pack(LF, 64, PKL, 32, 3, 3)
+    SXZ[...] = XF[:, pl.ds(48, 64, stride=8), :]
+    SLZ[:, pl.ds(0, 70), :] = LF[:, pl.ds(0, 70, stride=8), :]
+    slab_moves = [
+        Move(PKL.at[:, pl.ds(0, 24)], RKL.at[:, pl.ds(0, 24)], -1, 0),
+        Move(PKL.at[:, pl.ds(256, 24)], RKL.at[:, pl.ds(256, 24)], -1, 0),
+        Move(SLZ, RLZ, -1, 0),
+        Move(PKX.at[:, pl.ds(0, 24)], RKX.at[:, pl.ds(24, 24)], -1, 0),
+        Move(PKX.at[:, pl.ds(232, 24)], RKX.at[:, pl.ds(256, 24)], -1, 0),
+        Move(SXZ, RXZ, -1, 0),
+    ]
+    SL4[:, pl.ds(5, 70), :] = LF[:, pl.ds(4, 70, stride=8), :]
     slot_moves += send_slots(2, before=False)
+    slot_moves.append(Move(SL4, NL.at[1], -1, 0))
     E[2, :, pl.ds(8, 64), :] = XF[:, pl.ds(51, 64, stride=8), :]
 
     def repeat(half):
         return jnp.broadcast_to(half[:, :, 7:8], half.shape)
 
     finish(early)
+    finish(slab_moves)
     unpack(RKL, LF, 0, 35, 5, jnp.zeros_like)
-    finish(slab_moves)
     for move in row_moves:
         move.sent()
     unpack(RKX, XF, 3, 32, 8, repeat)
+
+    @pl.when(tm < n_tm - 1)
+    def _():
+        XF[:, pl.ds(52, 64, stride=8), :] = RXZ[...]
+        LF[:, pl.ds(4, 70, stride=8), :] = RLZ[:, pl.ds(0, 70), :]
 
     interior(1)
     finish(row_moves)
     take_rows(2)
     E[2, :, pl.ds(2, 6), :] = XF[:, pl.ds(3, 6, stride=8), :]
     E[2, :, pl.ds(72, 6), :] = XF[:, pl.ds(563, 6, stride=8), :]
+    finish(slot_moves)
     finish(corner_moves)
     unpack(RKX, XF, 0, 3, 3, repeat)
     unpack(RKX, XF, 35, 3, 3, repeat)
     ends(1)
-    finish(slot_moves)
     slots_beside(2, 1)
     edges(3)
     slot_moves = send_corners(3)
@@ -592,10 +618,10 @@
         E[3] = E[2]
 
     interior(1)
+    finish(slot_moves)
     finish(row_moves)
     take_rows(3)
     ends(1)
-    finish(slot_moves)
     slots_beside(3, 1)
     results = [
         pltpu.make_async_copy(XF.at[:, pl.ds(48, 512)], x_out, lsem.at[0]),
@@ -626,7 +652,7 @@
     states = arrays[0]
     slots, rows, lon = states.shape
     n_obs = arrays[5].shape[-1]
-    n_transfers = 44
+    n_transfers = 50
 
     def vmem(*shape, kind=F32):
         return pltpu.VMEM(shape, kind)
@@ -666,6 +692,10 @@
             vmem(2, 80, lon // 2),
             vmem(2, 304, lon // 2),
             vmem(2, 280, lon // 2),
+            vmem(2, 64, lon // 2),
+            vmem(2, 72, lon // 2),
+            vmem(2, 64, lon // 2),
+            vmem(2, 72, lon // 2),
             vmem(slots, rows, lon),
             vmem(slots, rows, lon),
             vmem(3, rows, lon),

time: 50 us -> 47.9 us (0.958)
  the two profiles are of different devices: /device:TPU:93 before, /device:TPU:227 now
where the time goes in v2:
time: 47.9 us; the launch traced here: 47.8 us
  Pallas kernels  47.2 us (99%)
  between operations  0.64 us (1%)
    pallas_call x1, Pallas kernels, body(): pl.pallas_call(functools.partial(weave, n_tm, n_lat, n_transfers), out_sh...  45 us
    pallas_call x1, Pallas kernels, body(): pl.pallas_call(unweave, out_shape=(shape, shape), in_specs=[pl.BlockSpec(...  2.19 us

profile of v2, /device:TPU:227, one launch (start us, length us, event | category | flops | bytes accessed | tf_op | source)
XLA Modules:
  0.0 47.8 jit_solution(8954105780443036564)
XLA Ops:
  0.6 45.0 %shard_map.122 = (f32[2,512,128]{2,1,0:T(8,128)}, f32[2,512,128]{2,1,0:T(8,128)}) custom-call(f32[8,64,256]{2,1,0:T(8,128)} %refs_0_.1, f32[8,64,256]{2,1,0:T(8,128)} %refs_1_.1, f32[64,256]{1,0:T(8,128)} %refs_2_.1, f32[64,256]{1,0:T(8,128)} %refs_3_.1, f32[64,256]{1,0:T(8,128)} %refs_4_.1, s32[8,1,1024]{2,1,0:T(1,128)} %refs_5_.1, f32[8,1,1024]{2,1,0:T(1,128)} %refs_6_.1, ...), custom_call_target="tpu_custom_call" | custom-call | tf_op jit(solution)/shard_map/pallas_call | solution.py:662
  45.6 2.2 %shard_map.123 = (f32[8,64,256]{2,1,0:T(8,128)}, f32[8,64,256]{2,1,0:T(8,128)}) custom-call(f32[2,512,128]{2,1,0:T(8,128)} %get-tuple-element.4.x_hbm, f32[2,512,128]{2,1,0:T(8,128)} %get-tuple-element.5.l_hbm), custom_call_target="tpu_custom_call" | custom-call | tf_op jit(solution)/shard_map/pallas_call | solution.py:713

commit v3 on v2

--- a/solution.py
+++ b/solution.py
@@ -634,18 +634,23 @@
     assert made[0] == n_transfers
 
 
-def unweave(x_hbm, l_hbm, x_out, l_out, x_ref, l_ref, sems):
-    copies = [
-        pltpu.make_async_copy(src, dst, sems.at[i])
-        for i, (src, dst) in enumerate(((x_hbm, x_ref), (l_hbm, l_ref)))
-    ]
-    for copy in copies:
+def unweave(x_hbm, l_hbm, x_out, l_out, x_ref, l_ref, x_laid, l_laid, sems):
+    refs = ((x_hbm, x_ref, x_laid, x_out), (l_hbm, l_ref, l_laid, l_out))
+    arriving = [
+        pltpu.make_async_copy(refs[i][0], refs[i][1], sems.at[i]) for i in range(2)
+    ]
+    for copy in arriving:
         copy.start()
-    for copy, ref, out in zip(copies, (x_ref, l_ref), (x_out, l_out)):
-        copy.wait()
+    leaving = []
+    for i, (_, ref, laid, out) in enumerate(refs):
+        arriving[i].wait()
         for s in range(8):
             x = ref[:, pl.ds(s, 64, stride=8), :]
-            out[s] = jnp.concatenate([x[0], x[1]], axis=1)
+            laid[s] = jnp.concatenate([x[0], x[1]], axis=1)
+        leaving.append(pltpu.make_async_copy(laid, out, sems.at[2 + i]))
+        leaving[i].start()
+    for copy in leaving:
+        copy.wait()
 
 
 def body(n_tm, n_lat, *arrays):
@@ -714,11 +719,13 @@
         unweave,
         out_shape=(shape, shape),
         in_specs=[pl.BlockSpec(memory_space=pltpu.HBM)] * 2,
-        out_specs=(pl.BlockSpec(memory_space=pltpu.VMEM),) * 2,
+        out_specs=(pl.BlockSpec(memory_space=pltpu.HBM),) * 2,
         scratch_shapes=[
             vmem(2, 512, lon // 2),
             vmem(2, 512, lon // 2),
-            pltpu.SemaphoreType.DMA((2,)),
+            vmem(slots, rows, lon),
+            vmem(slots, rows, lon),
+            pltpu.SemaphoreType.DMA((4,)),
         ],
         compiler_params=pltpu.CompilerParams(vmem_limit_bytes=64 * 1024 * 1024 - 65536),
     )(*fields)

time: 47.9 us -> 47.9 us (level)
  no operation moved by 1% of the time
where the time goes in v3:
time: 47.9 us; the launch traced here: 47.7 us
  Pallas kernels  47.1 us (98%)
  between operations  0.64 us (1%)
    pallas_call x1, Pallas kernels, body(): pl.pallas_call(functools.partial(weave, n_tm, n_lat, n_transfers), out_sh...  45 us
    pallas_call x1, Pallas kernels, body(): pl.pallas_call(unweave, out_shape=(shape, shape), in_specs=[pl.BlockSpec(...  2.14 us

profile of v3, /device:TPU:227, one launch (start us, length us, event | category | flops | bytes accessed | tf_op | source)
XLA Modules:
  0.0 47.7 jit_solution(16798780085555605043)
XLA Ops:
  0.6 45.0 %shard_map.122 = (f32[2,512,128]{2,1,0:T(8,128)}, f32[2,512,128]{2,1,0:T(8,128)}) custom-call(f32[8,64,256]{2,1,0:T(8,128)} %refs_0_.1, f32[8,64,256]{2,1,0:T(8,128)} %refs_1_.1, f32[64,256]{1,0:T(8,128)} %refs_2_.1, f32[64,256]{1,0:T(8,128)} %refs_3_.1, f32[64,256]{1,0:T(8,128)} %refs_4_.1, s32[8,1,1024]{2,1,0:T(1,128)} %refs_5_.1, f32[8,1,1024]{2,1,0:T(1,128)} %refs_6_.1, ...), custom_call_target="tpu_custom_call" | custom-call | tf_op jit(solution)/shard_map/pallas_call | solution.py:667
  45.6 2.1 %shard_map.123 = (f32[8,64,256]{2,1,0:T(8,128)}, f32[8,64,256]{2,1,0:T(8,128)}) custom-call(f32[2,512,128]{2,1,0:T(8,128)} %get-tuple-element.4.x_hbm, f32[2,512,128]{2,1,0:T(8,128)} %get-tuple-element.5.l_hbm), custom_call_target="tpu_custom_call" | custom-call | tf_op jit(solution)/shard_map/pallas_call | solution.py:718
